TPU v7x, 32 devices: a whole 2x2x4 slice. The times are simulated.
32 devices in a mesh: tm: 4 (over y, x), rows: 8 (over z, core).
Axes of the slice: x: 2, y: 2, z: 4, core: 2. Of those that a mesh axis runs over, the one named last changes fastest.
Arguments:
- features: bfloat16 [4, 8, 16, 96, 384], P(None, 'tm', 'rows'), may hold values from -6 to 6
- frame_counts: int32 [4], replicated, may hold values from 1 to 8, as said below
- owner_order: int32 [4], replicated, may hold values from 0 to 3, each once
- first_gain: float32 [384], replicated, may hold values from 0.1 to 1.9
- first_kernel: bfloat16 [3, 3, 3, 384, 384], replicated, may hold values from -0.0625 to 0.0625
- first_bias: float32 [384], replicated, may hold values from -3 to 3
- second_gain: float32 [384], replicated, may hold values from 0.1 to 1.9
- second_kernel: bfloat16 [3, 3, 3, 384, 384], replicated, may hold values from -0.0625 to 0.0625
- second_bias: float32 [384], replicated, may hold values from -3 to 3
Outputs:
- student_latents: bfloat16 [4, 8, 16, 96, 384], P('tm', None, None, 'rows')
Inputs may be any that keep to these rules, and one draw needn't show every extreme that they name: `frame_counts`: at least one clip has exactly 8 frames. `owner_order`: each clip appears once.
All inputs are finite; a program needn't handle non-finite values.
Results may differ from a plain program's by a relative error of at most 0.008.
Values may be sent and summed in bfloat16 or wider, within the bound.
No kernel may reach another device: no remote copies, remote signals or barrier semaphores. Data moves between devices by JAX's collectives and lax.ppermute only.
A program may use at most 128 MiB of HBM per device.

v0:
```python
import jax
import jax.numpy as jnp
import numpy as np
from jax import lax
from jax.experimental import pallas as pl
from jax.experimental.pallas import tpu as pltpu
from jax.sharding import PartitionSpec as P

EPSILON = 1e-06
HALO = 2
VMEM = 58 * 2**20
SCALARS = pl.BlockSpec(memory_space=pltpu.SMEM)
WHOLE = pl.BlockSpec(memory_space=pltpu.VMEM)
ANYWHERE = pl.BlockSpec(memory_space=pl.ANY)


def one_hot(source, columns):
    return jnp.asarray(
        (np.asarray(source)[..., None] == np.arange(columns)).astype(np.float32), jnp.bfloat16
    )


def permuted(table, rows):
    return jnp.dot(table, rows, preferred_element_type=jnp.float32).astype(jnp.bfloat16)


def pack(features, owner_order, wanted):
    clips, frames, height, width, channels = features.shape
    bands = len(wanted)
    band, rows = width // bands, frames * height * width
    columns = np.asarray(wanted) + np.arange(bands)[:, None] * band
    places = np.arange(frames * height) * width + columns[:, :, None]
    places = np.where(((columns >= 0) & (columns < width))[:, :, None], places, -1).reshape(-1)

    def kernel(order_ref, table_ref, features_ref, out_ref):
        for slot in range(clips):
            source = features_ref[order_ref[slot]]
            out_ref[slot] = permuted(table_ref[...], source)

    packed = pl.pallas_call(
        kernel,
        in_specs=[SCALARS, WHOLE, WHOLE],
        out_specs=WHOLE,
        out_shape=jax.ShapeDtypeStruct((clips, len(places), channels), features.dtype),
        compiler_params=pltpu.CompilerParams(vmem_limit_bytes=VMEM // 4),
    )(owner_order, one_hot(places, rows), features.reshape(clips, rows, channels))
    return packed.reshape(-1, channels)


def unpack_table(parts, first, columns, bands, frames, height):
    tables = []
    for kind, start in enumerate(first):
        places = np.full((frames, columns, bands, height), -1)
        base = 0
        for held in parts:
            count = len(held[kind])
            rows = np.arange(bands * count * frames * height) + base
            rows = rows.reshape(bands, count, frames, height).transpose(2, 1, 0, 3)
            for at, column in enumerate(held[kind]):
                places[:, column - start] = rows[:, at]
            base += bands * count * frames * height
        tables.append(places.reshape(-1))
    return one_hot(np.stack(tables), base)


def normalize(values, gain):
    factor = lax.rsqrt(jnp.mean(values * values, axis=-1, keepdims=True) + EPSILON)
    scaled = values * factor * gain
    return scaled / (1.0 + jnp.exp(-scaled))


def spread(active, taps_ref, frame, height):
    rows, channels = active.shape
    place = lax.rem(lax.broadcasted_iota(jnp.int32, (rows, 1), 0), height)
    above = jnp.where(place == 0, 0.0, pltpu.roll(active, 1, 0))
    below = jnp.where(place == height - 1, 0.0, pltpu.roll(active, rows - 1, 0))
    kept = rows - 2 * height
    for row_tap, shifted in enumerate((above, active, below)):
        narrow = shifted.astype(jnp.bfloat16)
        for column_tap in range(3):
            at = (row_tap * 3 + column_tap) * channels
            taps_ref[frame, :kept, at : at + channels] = narrow[
                column_tap * height : column_tap * height + kept
            ]


def group(frames, rows):
    return max(g for g in range(1, frames + 1) if frames % g == 0 and (g == 1 or g * rows <= 640))


def multiply(taps_ref, weights_ref, copies, near_ref, far_ref, rows, channels):
    frames, _, taps = taps_ref.shape
    near_ref[0, :rows] = jnp.zeros((rows, 2 * channels), jnp.float32)
    far_ref[:2, :rows] = jnp.zeros((2, rows, channels), jnp.float32)

    def dots(count, sums_ref, skip, start, width):
        size = group(count, rows)

        @pl.loop(0, count // size)
        def _(step):
            operand = taps_ref[pl.ds(step * size, size), :rows].reshape(size * rows, taps)
            sums = jnp.dot(
                operand, weights_ref[:, start : start + width], preferred_element_type=jnp.float32
            )
            sums_ref[pl.ds(step * size + skip, size), :rows] = sums.reshape(size, rows, width)

    copies[0].wait()
    copies[1].wait()
    dots(frames, near_ref, 1, 0, 2 * channels)
    copies[2].wait()
    dots(frames - 2, far_ref, 2, 2 * channels, channels)


def added(near_ref, far_ref, frame, rows, channels):
    return (
        near_ref[frame + 1, :rows, :channels]
        + near_ref[frame, :rows, channels:]
        + far_ref[frame, :rows]
    )


def stage(
    owner_order,
    frame_counts,
    sources,
    table,
    saved,
    earlier,
    kernels,
    vectors,
    *,
    band,
    height,
    columns,
    new_at,
    saved_at,
    keep_at,
    center_at,
    out_at,
    edges,
    earlier_at=None,
):
    slabs, _, channels = sources[0].shape
    kinds, unpacked, _ = table.shape
    frames = slabs * (unpacked // (columns * height))
    taps = 9 * channels
    fresh = columns - 2
    window = fresh + (HALO if saved is not None else 0)
    made = window - 2
    inner, outer = fresh * height, made * height
    keeps, joins = keep_at is not None, earlier is not None

    def kernel(*refs):
        refs = list(refs)
        order_ref, counts_ref = refs.pop(0), refs.pop(0)
        source_refs = [refs.pop(0) for _ in sources]
        table_ref = refs.pop(0)
        saved_ref = refs.pop(0) if saved is not None else None
        earlier_ref = refs.pop(0) if joins else None
        kernel_refs = [refs.pop(0), refs.pop(0)]
        first_gain, first_bias, second_gain, second_bias = (refs.pop(0) for _ in range(4))
        out_ref = refs.pop(0)
        kept_ref = refs.pop(0) if keeps else None
        weights_refs = [refs.pop(0), refs.pop(0)]
        raw_ref, taps_ref, near_ref, far_ref, active_ref, arrived = refs[:6]
        result_ref, written = refs[6:] if joins else (out_ref, None)

        copies = [
            [
                pltpu.make_async_copy(
                    source.at[2 - ahead],
                    weights.at[:, pl.ds(ahead * channels, channels)],
                    arrived.at[which, ahead],
                )
                for ahead in range(3)
            ]
            for which, (source, weights) in enumerate(zip(kernel_refs, weights_refs))
        ]
        for copy in copies[0] + copies[1]:
            copy.start()

        at = lax.axis_index("rows")
        kind = lax.rem(at, kinds)

        def pick(places):
            return jnp.where(kind == 0, places[0], places[-1])

        moved = None
        if joins:
            moved = pltpu.make_async_copy(
                earlier_ref,
                out_ref.at[:, pl.ds(pick(earlier_at), earlier.shape[1])],
                written.at[frames],
            )
            moved.start()
        count = counts_ref[order_ref[lax.axis_index("tm")]]
        first_edge = edges & (at == 0)
        last_edge = edges & (at == lax.axis_size("rows") - 1)

        @pl.loop(0, slabs)
        def _(slab):
            rows = jnp.concatenate([source[slab] for source in source_refs], axis=0)
            placed = permuted(table_ref[kind], rows).reshape(-1, columns, height, channels)
            raw_ref[pl.ds(slab * placed.shape[0], placed.shape[0])] = placed

        @pl.loop(0, frames)
        def _(frame):
            values = raw_ref[frame].reshape(columns * height, channels).astype(jnp.float32)
            spread(normalize(values, first_gain[...]), taps_ref, frame, height)

        multiply(taps_ref, weights_refs[0], copies[0], near_ref, far_ref, inner, channels)
        place = lax.broadcasted_iota(jnp.int32, (inner, 1), 0)
        outside = ((place < height) & first_edge) | ((place >= inner - height) & last_edge)

        @pl.loop(0, frames)
        def _(frame):
            hidden = added(near_ref, far_ref, frame, inner, channels) + first_bias[...]
            hidden = hidden.astype(jnp.bfloat16).astype(jnp.float32)
            active = jnp.where(outside, 0.0, normalize(hidden, second_gain[...]))
            if saved is not None or keeps:
                active = active.reshape(fresh, height, channels)
                active_ref[pl.ds(pick(new_at), fresh)] = active
                if saved is not None:
                    active_ref[pl.ds(pick(saved_at), HALO)] = saved_ref[frame].astype(jnp.float32)
                if keeps:
                    kept = active_ref[pl.ds(pick(keep_at), HALO)]
                    kept_ref[frame] = kept.astype(jnp.bfloat16)
                active = active_ref[...].reshape(window * height, channels)
            spread(active, taps_ref, frame, height)

        multiply(taps_ref, weights_refs[1], copies[1], near_ref, far_ref, outer, channels)

        def write(frame):
            return pltpu.make_async_copy(
                result_ref.at[frame],
                out_ref.at[frame, pl.ds(pick(out_at), made)],
                written.at[frame],
            )

        @pl.loop(0, frames)
        def _(frame):
            center = raw_ref[frame, pl.ds(pick(center_at), made)].reshape(outer, channels)
            result = added(near_ref, far_ref, frame, outer, channels) + second_bias[...]
            result = result + center.astype(jnp.float32)
            result = jnp.where(frame < count, result, 0.0).astype(jnp.bfloat16)
            result_ref[frame] = result.reshape(made, height, channels)
            if joins:
                write(frame).start()

        if joins:
            moved.wait()

            @pl.loop(0, frames)
            def _(frame):
                write(frame).wait()

    out_shape = [
        jax.ShapeDtypeStruct((frames, band if joins else made, height, channels), jnp.bfloat16)
    ]
    if keeps:
        out_shape.append(jax.ShapeDtypeStruct((frames, HALO, height, channels), jnp.bfloat16))
    operands = [owner_order, frame_counts, *sources, table]
    specs = [SCALARS] * 2 + [WHOLE] * (len(sources) + 1)
    if saved is not None:
        operands.append(saved)
        specs.append(WHOLE)
    if joins:
        operands.append(earlier)
        specs.append(ANYWHERE)
    most = max(inner, outer)
    scratch = [
        pltpu.VMEM((taps, 3 * channels), jnp.bfloat16),
        pltpu.VMEM((taps, 3 * channels), jnp.bfloat16),
        pltpu.VMEM((frames, columns, height, channels), jnp.bfloat16),
        pltpu.VMEM((frames, most, taps), jnp.bfloat16),
        pltpu.VMEM((frames + 1, most, 2 * channels), jnp.float32),
        pltpu.VMEM((frames, most, channels), jnp.float32),
        pltpu.VMEM((window, height, channels), jnp.float32),
        pltpu.SemaphoreType.DMA((2, 3)),
    ]
    if joins:
        scratch += [
            pltpu.VMEM((frames, made, height, channels), jnp.bfloat16),
            pltpu.SemaphoreType.DMA((frames + 1,)),
        ]
    flops = 2 * 3 * taps * channels * frames * (inner + outer)
    return pl.pallas_call(
        kernel,
        in_specs=specs + [ANYWHERE] * 2 + [WHOLE] * 4,
        out_specs=[ANYWHERE if joins else WHOLE] + [WHOLE] * keeps,
        out_shape=out_shape,
        scratch_shapes=scratch,
        compiler_params=pltpu.CompilerParams(vmem_limit_bytes=VMEM),
        cost_estimate=pl.CostEstimate(flops=flops, bytes_accessed=20 * 2**20, transcendentals=0),
    )(*operands, *kernels, *vectors)


def exchange(packed):
    return lax.all_to_all(packed, ("tm", "rows"), split_axis=0, concat_axis=0, tiled=True)


def per_device(
    features,
    frame_counts,
    owner_order,
    first_gain,
    first_kernel,
    first_bias,
    second_gain,
    second_kernel,
    second_bias,
):
    slabs, bands = lax.axis_size("tm"), lax.axis_size("rows")
    frames, height = features.shape[1:3]
    channels = features.shape[4]
    band = features.shape[3] // bands
    cells = frames * height
    kernels = [k.reshape(3, 9 * channels, channels) for k in (first_kernel, second_kernel)]
    vectors = [
        v.reshape(1, channels) for v in (first_gain, first_bias, second_gain, second_bias)
    ]

    def slabbed(rows):
        return rows.reshape(slabs, -1, channels)

    def columns_of(received, count, start, stop):
        rows = received.reshape(slabs * bands, count * cells, channels)
        return rows[:, start * cells : stop * cells].reshape(-1, channels)

    common = dict(band=band, height=bands * height)
    later = band // 3
    if later >= HALO and bands % 2 == 0:
        soon = band - later
        order = (list(range(band - 1, -1 - HALO, -1)), list(range(band + HALO)))
        early = [columns[:soon] for columns in order]
        late = [columns[soon:] for columns in order]
        shared = [list(range(band, band + HALO)), list(range(-1, -1 - HALO, -1))]
        middle = [columns[-HALO:] for columns in early]
        wide, rest = soon + HALO, later + 2 * HALO

        received = exchange(pack(features, owner_order, [early[i % 2] for i in range(bands)]))
        packed = pack(features, owner_order, [late[i % 2] for i in range(bands)])
        received, packed = lax.optimization_barrier((received, packed))
        received_late = exchange(packed)
        halo = lax.ppermute(
            columns_of(received, soon, 0, HALO), "rows", [(i, i ^ 1) for i in range(bands)]
        )
        half, kept = stage(
            owner_order,
            frame_counts,
            [slabbed(received), slabbed(halo)],
            unpack_table((early, shared), (later, -HALO), wide, bands, frames, height),
            None,
            None,
            kernels,
            vectors,
            columns=wide,
            new_at=(0, 0),
            saved_at=None,
            keep_at=(0, soon - HALO),
            center_at=(2, 2),
            out_at=(later + 2, 0),
            edges=False,
            **common,
        )
        (result,) = stage(
            owner_order,
            frame_counts,
            [slabbed(received_late), slabbed(columns_of(received, soon, soon - HALO, soon))],
            unpack_table((late, middle), (-HALO, soon - HALO), rest, bands, frames, height),
            kept,
            half,
            kernels,
            vectors,
            columns=rest,
            new_at=(0, HALO),
            saved_at=(later + 2, 0),
            keep_at=None,
            center_at=(HALO, 0),
            out_at=(0, soon - 2),
            earlier_at=(later + 2, 0),
            edges=True,
            **common,
        )
    else:
        own = list(range(band))
        received = exchange(pack(features, owner_order, [own] * bands))
        up = [(i, i + 1) for i in range(bands - 1)]
        left = lax.ppermute(columns_of(received, band, band - HALO, band), "rows", up)
        right = lax.ppermute(columns_of(received, band, 0, HALO), "rows", [(j, i) for i, j in up])
        held = ([own], [list(range(-HALO, 0))], [list(range(band, band + HALO))])
        (result,) = stage(
            owner_order,
            frame_counts,
            [slabbed(received), slabbed(left), slabbed(right)],
            unpack_table(held, (-HALO,), band + 2 * HALO, bands, frames, height),
            None,
            None,
            kernels,
            vectors,
            columns=band + 2 * HALO,
            new_at=(0,),
            saved_at=None,
            keep_at=None,
            center_at=(HALO,),
            out_at=(0,),
            edges=True,
            **common,
        )
    return result.transpose(0, 2, 1, 3)[None]


def solution(mesh):
    placed = (P(None, "tm", "rows", None, None), P(), P(), P(), P(), P(), P(), P(), P())
    return jax.shard_map(
        per_device,
        mesh=mesh,
        in_specs=placed,
        out_specs=P("tm", None, None, "rows", None),
        check_vma=False,
    )
```

profile of v0, /device:TPU:0, one launch (start us, length us, event | category | flops | bytes accessed | tf_op | source)
XLA Modules:
  0.0 88.7 jit_solution(6603370268988650969)
XLA Ops:
  0.0 0.0 copy-start
  0.0 1.3 %copy-done = bf16[4,2,2,96,384]{4,3,2,1,0:T(8,128)(2,1)S(1)} copy-done((bf16[4,2,2,96,384]{4,3,2,1,0:T(8,128)(2,1)S(1)}, bf16[4,2,2,96,384]{4,3,2,1,0:T(8,128)(2,1)}, u32[]{:S(2)}) %copy-start) | copy-done | bytes 1179672
  1.3 0.0 copy-start.2
  1.3 0.9 %copy-done.2 = bf16[256,384]{1,0:T(8,128)(2,1)S(1)} copy-done((bf16[256,384]{1,0:T(8,128)(2,1)S(1)}, bf16[256,384]{1,0:T(8,128)(2,1)}, u32[]{:S(2)}) %copy-start.2) | copy-done | bytes 196632
  2.2 0.0 copy-start.4
  2.2 0.7 copy-done.4
  2.9 2.1 %shard_map.127 = bf16[4,256,384]{2,1,0:T(8,128)(2,1)} custom-call(s32[4]{0:T(128)S(1)} %copy-done.4, bf16[256,384]{1,0:T(8,128)(2,1)S(1)} %copy-done.2, bf16[4,384,384]{2,1,0:T(8,128)(2,1)S(1)} %bitcast.17), custom_call_target="tpu_custom_call" | custom-call | tf_op jit(solution)/shard_map/pallas_call | solution.py:40
  4.9 7.3 %all-to-all-start = ((bf16[32,32,384]{2,1,0:T(8,128)(2,1)}), bf16[32,32,384]{2,1,0:T(8,128)(2,1)S(1)}, u32[]{:S(2)}, u32[]{:S(2)}) async-start(bf16[32,32,384]{2,1,0:T(8,128)(2,1)} %bitcast.1), calls=%async_computation | async-start | bytes 1572864 | tf_op jit(solution)/shard_map/all_to_all | solution.py:299
  12.2 0.0 copy-start.1
  12.2 1.3 %copy-done.1 = bf16[4,2,2,96,384]{4,3,2,1,0:T(8,128)(2,1)S(1)} copy-done((bf16[4,2,2,96,384]{4,3,2,1,0:T(8,128)(2,1)S(1)}, bf16[4,2,2,96,384]{4,3,2,1,0:T(8,128)(2,1)}, u32[]{:S(2)}) %copy-start.1) | copy-done | bytes 1179672
  13.5 0.0 copy-start.3
  13.5 0.9 %copy-done.3 = bf16[192,384]{1,0:T(8,128)(2,1)S(1)} copy-done((bf16[192,384]{1,0:T(8,128)(2,1)S(1)}, bf16[192,384]{1,0:T(8,128)(2,1)}, u32[]{:S(2)}) %copy-start.3) | copy-done | bytes 147480
  14.4 0.0 copy-start.5
  14.4 0.7 copy-done.5
  15.1 1.9 %shard_map.128 = bf16[4,192,384]{2,1,0:T(8,128)(2,1)} custom-call(s32[4]{0:T(128)S(1)} %copy-done.5, bf16[192,384]{1,0:T(8,128)(2,1)S(1)} %copy-done.3, bf16[4,384,384]{2,1,0:T(8,128)(2,1)S(1)} %bitcast.18), custom_call_target="tpu_custom_call" | custom-call | tf_op jit(solution)/shard_map/pallas_call | solution.py:40
  16.9 17.2 %all-to-all-done = bf16[32,32,384]{2,1,0:T(8,128)(2,1)S(1)} async-done(((bf16[32,32,384]{2,1,0:T(8,128)(2,1)}), bf16[32,32,384]{2,1,0:T(8,128)(2,1)S(1)}, u32[]{:S(2)}, u32[]{:S(2)}) %all-to-all-start) | async-done | bytes 786464 | tf_op jit(solution)/shard_map/all_to_all | solution.py:299
  34.2 0.0 copy-start.6
  34.2 0.8 slice_bitcast_fusion
  35.0 0.0 collective-permute-start
  35.0 1.3 %reshape.57.refs_7_.refs_9_ = f32[1,384]{1,0:T(1,128)} reshape(f32[384]{0:T(512)} %param.16) | data formatting | bytes 3072 | tf_op jit(solution)/shard_map/reshape | solution.py:320
  36.2 1.3 %reshape.58.refs_8_.refs_10_ = f32[1,384]{1,0:T(1,128)} reshape(f32[384]{0:T(512)} %param.18) | data formatting | bytes 3072 | tf_op jit(solution)/shard_map/reshape | solution.py:320
  37.5 1.3 %reshape.59.refs_9_.refs_11_ = f32[1,384]{1,0:T(1,128)} reshape(f32[384]{0:T(512)} %param.19) | data formatting | bytes 3072 | tf_op jit(solution)/shard_map/reshape | solution.py:320
  38.8 1.3 %reshape.60.refs_10_.refs_12_ = f32[1,384]{1,0:T(1,128)} reshape(f32[384]{0:T(512)} %param.21) | data formatting | bytes 3072 | tf_op jit(solution)/shard_map/reshape | solution.py:320
  40.0 2.6 %all-to-all-start.1 = ((bf16[32,24,384]{2,1,0:T(8,128)(2,1)}), bf16[32,24,384]{2,1,0:T(8,128)(2,1)S(1)}, u32[]{:S(2)}, u32[]{:S(2)}) async-start(bf16[32,24,384]{2,1,0:T(8,128)(2,1)} %bitcast.4), calls=%async_computation.1 | async-start | bytes 1179648 | tf_op jit(solution)/shard_map/all_to_all | solution.py:299
  42.7 0.0 collective-permute-done
  42.7 0.0 copy-start.8
  42.7 0.0 copy-done.6
  42.7 0.7 copy-done.8
  43.3 23.7 %shard_map.129 = (bf16[8,6,16,384]{3,2,1,0:T(8,128)(2,1)}, bf16[8,2,16,384]{3,2,1,0:T(8,128)(2,1)}) custom-call(s32[4]{0:T(128)} %refs_0_.3, s32[4]{0:T(128)} %refs_1_.3, bf16[4,256,384]{2,1,0:T(8,128)(2,1)} %bitcast.19, bf16[4,64,384]{2,1,0:T(8,128)(2,1)} %bitcast.26, bf16[2,320,320]{2,1,0:T(8,128)(2,1)} %constant.10.clone.refs_4_, ...), custom_call_target="tpu_custom_call" | custom-call | flops 14269022208 | bytes 20971520 | tf_op jit(solution)/shard_map/pallas_call | solution.py:287
  67.0 0.0 all-to-all-done.1
  67.0 0.0 copy-start.7
  67.1 0.8 copy-done.7
  67.9 20.8 %shard_map.130 = bf16[8,12,16,384]{3,2,1,0:T(8,128)(2,1)} custom-call(s32[4]{0:T(128)} %refs_0_.3, s32[4]{0:T(128)} %refs_1_.3, bf16[4,192,384]{2,1,0:T(8,128)(2,1)} %bitcast.20, bf16[4,64,384]{2,1,0:T(8,128)(2,1)} %bitcast.21, bf16[2,256,256]{2,1,0:T(8,128)(2,1)} %constant.11.clone.refs_4_, bf16[8,2,16,384]{3,2,1,0:T(8,128)(2,1)} %get-tuple-element.11.refs_5_, ...), custom_call_target="tpu_custom_call" | custom-call | flops 12230590464 | bytes 20971520 | tf_op jit(solution)/shard_map/pallas_call | solution.py:287
Async XLA Ops:
  0.0 1.3 %copy-start = (bf16[4,2,2,96,384]{4,3,2,1,0:T(8,128)(2,1)S(1)}, bf16[4,2,2,96,384]{4,3,2,1,0:T(8,128)(2,1)}, u32[]{:S(2)}) copy-start(bf16[4,2,2,96,384]{4,3,2,1,0:T(8,128)(2,1)} %param.13) | copy-start | bytes 3538948
  1.3 0.9 %copy-start.2 = (bf16[256,384]{1,0:T(8,128)(2,1)S(1)}, bf16[256,384]{1,0:T(8,128)(2,1)}, u32[]{:S(2)}) copy-start(bf16[256,384]{1,0:T(8,128)(2,1)} %constant.8.clone.table_ref) | copy-start | bytes 589828
  2.2 0.7 copy-start.4
  4.9 29.3 %all-to-all-start = ((bf16[32,32,384]{2,1,0:T(8,128)(2,1)}), bf16[32,32,384]{2,1,0:T(8,128)(2,1)S(1)}, u32[]{:S(2)}, u32[]{:S(2)}) async-start(bf16[32,32,384]{2,1,0:T(8,128)(2,1)} %bitcast.1), calls=%async_computation | async-start | bytes 1572864 | tf_op jit(solution)/shard_map/all_to_all | solution.py:299
  12.2 1.3 %copy-start.1 = (bf16[4,2,2,96,384]{4,3,2,1,0:T(8,128)(2,1)S(1)}, bf16[4,2,2,96,384]{4,3,2,1,0:T(8,128)(2,1)}, u32[]{:S(2)}) copy-start(bf16[4,2,2,96,384]{4,3,2,1,0:T(8,128)(2,1)} %param.13) | copy-start | bytes 3538948
  13.5 0.9 %copy-start.3 = (bf16[192,384]{1,0:T(8,128)(2,1)S(1)}, bf16[192,384]{1,0:T(8,128)(2,1)}, u32[]{:S(2)}) copy-start(bf16[192,384]{1,0:T(8,128)(2,1)} %constant.9.clone.table_ref) | copy-start | bytes 442372
  14.4 0.7 copy-start.5
  34.2 8.5 %copy-start.6 = (bf16[32,32,384]{2,1,0:T(8,128)(2,1)}, bf16[32,32,384]{2,1,0:T(8,128)(2,1)S(1)}, u32[]{:S(2)}) copy-start(bf16[32,32,384]{2,1,0:T(8,128)(2,1)S(1)} %all-to-all-done) | copy-start | bytes 2359300
  35.0 7.7 %collective-permute-start = (bf16[256,384]{1,0:T(8,128)(2,1)S(1)}, bf16[256,384]{1,0:T(8,128)(2,1)S(1)}, u32[]{:S(2)}, u32[]{:S(2)}) collective-permute-start(bf16[256,384]{1,0:T(8,128)(2,1)S(1)} %get-tuple-element.13), channel_id=1, source_target_pairs={{0,1},{1,0},{2,3},{3,2},{4,5},{5,4},{6,7},{7,6},{8,9},{9,8},{10,11... | collective-permute-start | bytes 589832 | tf_op jit(solution)/shard_map/ppermute | solution.py:345
  40.0 27.0 %all-to-all-start.1 = ((bf16[32,24,384]{2,1,0:T(8,128)(2,1)}), bf16[32,24,384]{2,1,0:T(8,128)(2,1)S(1)}, u32[]{:S(2)}, u32[]{:S(2)}) async-start(bf16[32,24,384]{2,1,0:T(8,128)(2,1)} %bitcast.4), calls=%async_computation.1 | async-start | bytes 1179648 | tf_op jit(solution)/shard_map/all_to_all | solution.py:299
  42.7 0.7 copy-start.8
  67.0 0.8 copy-start.7
where the time goes:
time: 89.3 us; the launch traced here: 88.7 us
  Pallas kernels  48.5 us (54%)
  waiting for transfers between devices  17.2 us (19%)
  local copies, waits for them, and re-layouts  13 us (15%)
  starting transfers between devices  9.91 us (11%)
    pallas_call x2, Pallas kernels, stage(): pl.pallas_call(kernel, in_specs=specs + [ANYWHERE] * 2 + [WHOLE] * 4, out...  44.5 us
    all_to_all x2, waiting for transfers between devices, exchange(): lax.all_to_all(packed, ('tm', 'rows'), split_axis=0, concat_axis=0, tiled...  17.2 us
    all_to_all x2, starting transfers between devices, exchange(): lax.all_to_all(packed, ('tm', 'rows'), split_axis=0, concat_axis=0, tiled...  9.91 us
    unnamed x18, local copies, waits for them, and re-layouts  7.15 us
    reshape x4, local copies, waits for them, and re-layouts, per_device(): v.reshape(1, channels)  5.06 us
    pallas_call x2, Pallas kernels, pack(): pl.pallas_call(kernel, in_specs=[SCALARS, WHOLE, WHOLE], out_specs=WHOLE,...  3.94 us
  transfers between devices with their start and end apart: 3, of which 1 were waited for; matrix products, arithmetic and copies ran while one was open for 6% of the time, Pallas kernels for 29%

commit v1 on v0

--- a/solution.py
+++ b/solution.py
@@ -9,7 +9,7 @@
 EPSILON = 1e-06
 HALO = 2
 VMEM = 58 * 2**20
-SCALARS = pl.BlockSpec(memory_space=pltpu.SMEM)
+SPARE = 19 * 2**20
 WHOLE = pl.BlockSpec(memory_space=pltpu.VMEM)
 ANYWHERE = pl.BlockSpec(memory_space=pl.ANY)
 
@@ -32,17 +32,36 @@
     places = np.arange(frames * height) * width + columns[:, :, None]
     places = np.where(((columns >= 0) & (columns < width))[:, :, None], places, -1).reshape(-1)
 
-    def kernel(order_ref, table_ref, features_ref, out_ref):
-        for slot in range(clips):
-            source = features_ref[order_ref[slot]]
-            out_ref[slot] = permuted(table_ref[...], source)
+    def kernel(order_ref, table_ref, features_ref, out_ref, table, sources, arrived):
+        fetched = pltpu.make_async_copy(table_ref, table, arrived.at[clips])
+        copies = [
+            pltpu.make_async_copy(
+                features_ref.at[order_ref[slot]], sources.at[slot], arrived.at[slot]
+            )
+            for slot in range(clips)
+        ]
+        for copy in [fetched] + copies:
+            copy.start()
+        fetched.wait()
+        for slot, copy in enumerate(copies):
+            copy.wait()
+            out_ref[slot] = permuted(table[...], sources[slot])
 
     packed = pl.pallas_call(
         kernel,
-        in_specs=[SCALARS, WHOLE, WHOLE],
-        out_specs=WHOLE,
+        grid_spec=pltpu.PrefetchScalarGridSpec(
+            num_scalar_prefetch=1,
+            grid=(1,),
+            in_specs=[ANYWHERE] * 2,
+            out_specs=WHOLE,
+            scratch_shapes=[
+                pltpu.VMEM((len(places), rows), jnp.bfloat16),
+                pltpu.VMEM((clips, rows, channels), jnp.bfloat16),
+                pltpu.SemaphoreType.DMA((clips + 1,)),
+            ],
+        ),
         out_shape=jax.ShapeDtypeStruct((clips, len(places), channels), features.dtype),
-        compiler_params=pltpu.CompilerParams(vmem_limit_bytes=VMEM // 4),
+        compiler_params=pltpu.CompilerParams(vmem_limit_bytes=VMEM),
     )(owner_order, one_hot(places, rows), features.reshape(clips, rows, channels))
     return packed.reshape(-1, channels)
 
@@ -60,7 +79,7 @@
                 places[:, column - start] = rows[:, at]
             base += bands * count * frames * height
         tables.append(places.reshape(-1))
-    return one_hot(np.stack(tables), base)
+    return one_hot(np.stack(tables), -(-base // 128) * 128)
 
 
 def normalize(values, gain):
@@ -120,8 +139,7 @@
 
 
 def stage(
-    owner_order,
-    frame_counts,
+    scalars,
     sources,
     table,
     saved,
@@ -141,7 +159,7 @@
     earlier_at=None,
 ):
     slabs, _, channels = sources[0].shape
-    kinds, unpacked, _ = table.shape
+    unpacked = table.shape[0]
     frames = slabs * (unpacked // (columns * height))
     taps = 9 * channels
     fresh = columns - 2
@@ -152,18 +170,21 @@
 
     def kernel(*refs):
         refs = list(refs)
-        order_ref, counts_ref = refs.pop(0), refs.pop(0)
+        scalars_ref = refs.pop(0)
         source_refs = [refs.pop(0) for _ in sources]
         table_ref = refs.pop(0)
         saved_ref = refs.pop(0) if saved is not None else None
         earlier_ref = refs.pop(0) if joins else None
         kernel_refs = [refs.pop(0), refs.pop(0)]
-        first_gain, first_bias, second_gain, second_bias = (refs.pop(0) for _ in range(4))
+        vectors_ref = refs.pop(0)
+        first_gain, first_bias, second_gain, second_bias = (
+            vectors_ref[i : i + 1] for i in range(4)
+        )
         out_ref = refs.pop(0)
         kept_ref = refs.pop(0) if keeps else None
         weights_refs = [refs.pop(0), refs.pop(0)]
         raw_ref, taps_ref, near_ref, far_ref, active_ref, arrived = refs[:6]
-        result_ref, written = refs[6:] if joins else (out_ref, None)
+        result_ref, held_ref, written = refs[6:] if joins else (out_ref, None, None)
 
         copies = [
             [
@@ -180,33 +201,38 @@
             copy.start()
 
         at = lax.axis_index("rows")
-        kind = lax.rem(at, kinds)
+        kind = lax.rem(at, 2)
 
         def pick(places):
             return jnp.where(kind == 0, places[0], places[-1])
 
-        moved = None
         if joins:
+            held = pltpu.make_async_copy(earlier_ref, held_ref, written.at[frames + 1])
+            held.start()
             moved = pltpu.make_async_copy(
-                earlier_ref,
+                held_ref,
                 out_ref.at[:, pl.ds(pick(earlier_at), earlier.shape[1])],
                 written.at[frames],
             )
-            moved.start()
-        count = counts_ref[order_ref[lax.axis_index("tm")]]
+        clips = scalars.shape[0] // 2
+        count = scalars_ref[clips + scalars_ref[lax.axis_index("tm")]]
         first_edge = edges & (at == 0)
         last_edge = edges & (at == lax.axis_size("rows") - 1)
 
         @pl.loop(0, slabs)
         def _(slab):
-            rows = jnp.concatenate([source[slab] for source in source_refs], axis=0)
-            placed = permuted(table_ref[kind], rows).reshape(-1, columns, height, channels)
+            rows = [source[slab] for source in source_refs]
+            spare = table_ref.shape[1] - sum(part.shape[0] for part in rows)
+            if spare:
+                rows.append(jnp.zeros((spare, channels), jnp.bfloat16))
+            rows = jnp.concatenate(rows, axis=0)
+            placed = permuted(table_ref[...], rows).reshape(-1, columns, height, channels)
             raw_ref[pl.ds(slab * placed.shape[0], placed.shape[0])] = placed
 
         @pl.loop(0, frames)
         def _(frame):
             values = raw_ref[frame].reshape(columns * height, channels).astype(jnp.float32)
-            spread(normalize(values, first_gain[...]), taps_ref, frame, height)
+            spread(normalize(values, first_gain), taps_ref, frame, height)
 
         multiply(taps_ref, weights_refs[0], copies[0], near_ref, far_ref, inner, channels)
         place = lax.broadcasted_iota(jnp.int32, (inner, 1), 0)
@@ -214,9 +240,9 @@
 
         @pl.loop(0, frames)
         def _(frame):
-            hidden = added(near_ref, far_ref, frame, inner, channels) + first_bias[...]
+            hidden = added(near_ref, far_ref, frame, inner, channels) + first_bias
             hidden = hidden.astype(jnp.bfloat16).astype(jnp.float32)
-            active = jnp.where(outside, 0.0, normalize(hidden, second_gain[...]))
+            active = jnp.where(outside, 0.0, normalize(hidden, second_gain))
             if saved is not None or keeps:
                 active = active.reshape(fresh, height, channels)
                 active_ref[pl.ds(pick(new_at), fresh)] = active
@@ -228,6 +254,9 @@
                 active = active_ref[...].reshape(window * height, channels)
             spread(active, taps_ref, frame, height)
 
+        if joins:
+            held.wait()
+            moved.start()
         multiply(taps_ref, weights_refs[1], copies[1], near_ref, far_ref, outer, channels)
 
         def write(frame):
@@ -240,7 +269,7 @@
         @pl.loop(0, frames)
         def _(frame):
             center = raw_ref[frame, pl.ds(pick(center_at), made)].reshape(outer, channels)
-            result = added(near_ref, far_ref, frame, outer, channels) + second_bias[...]
+            result = added(near_ref, far_ref, frame, outer, channels) + second_bias
             result = result + center.astype(jnp.float32)
             result = jnp.where(frame < count, result, 0.0).astype(jnp.bfloat16)
             result_ref[frame] = result.reshape(made, height, channels)
@@ -259,8 +288,8 @@
     ]
     if keeps:
         out_shape.append(jax.ShapeDtypeStruct((frames, HALO, height, channels), jnp.bfloat16))
-    operands = [owner_order, frame_counts, *sources, table]
-    specs = [SCALARS] * 2 + [WHOLE] * (len(sources) + 1)
+    operands = [scalars, *sources, table]
+    specs = [WHOLE] * (len(sources) + 1)
     if saved is not None:
         operands.append(saved)
         specs.append(WHOLE)
@@ -281,18 +310,28 @@
     if joins:
         scratch += [
             pltpu.VMEM((frames, made, height, channels), jnp.bfloat16),
-            pltpu.SemaphoreType.DMA((frames + 1,)),
+            pltpu.VMEM(earlier.shape, jnp.bfloat16),
+            pltpu.SemaphoreType.DMA((frames + 2,)),
         ]
+    held = sum(
+        int(np.prod(ref.shape)) * jnp.dtype(ref.dtype).itemsize
+        for ref in scratch
+        if len(ref.shape) > 2 or ref.shape[0] == taps
+    )
     flops = 2 * 3 * taps * channels * frames * (inner + outer)
     return pl.pallas_call(
         kernel,
-        in_specs=specs + [ANYWHERE] * 2 + [WHOLE] * 4,
-        out_specs=[ANYWHERE if joins else WHOLE] + [WHOLE] * keeps,
+        grid_spec=pltpu.PrefetchScalarGridSpec(
+            num_scalar_prefetch=1,
+            grid=(1,),
+            in_specs=specs + [ANYWHERE] * 2 + [WHOLE],
+            out_specs=[ANYWHERE if joins else WHOLE] + [WHOLE] * keeps,
+            scratch_shapes=scratch,
+        ),
         out_shape=out_shape,
-        scratch_shapes=scratch,
-        compiler_params=pltpu.CompilerParams(vmem_limit_bytes=VMEM),
+        compiler_params=pltpu.CompilerParams(vmem_limit_bytes=min(VMEM, held + SPARE)),
         cost_estimate=pl.CostEstimate(flops=flops, bytes_accessed=20 * 2**20, transcendentals=0),
-    )(*operands, *kernels, *vectors)
+    )(*operands, *kernels, vectors)
 
 
 def exchange(packed):
@@ -316,9 +355,8 @@
     band = features.shape[3] // bands
     cells = frames * height
     kernels = [k.reshape(3, 9 * channels, channels) for k in (first_kernel, second_kernel)]
-    vectors = [
-        v.reshape(1, channels) for v in (first_gain, first_bias, second_gain, second_bias)
-    ]
+    vectors = jnp.stack([first_gain, first_bias, second_gain, second_bias])
+    scalars = jnp.concatenate([owner_order, frame_counts])
 
     def slabbed(rows):
         return rows.reshape(slabs, -1, channels)
@@ -340,16 +378,24 @@
 
         received = exchange(pack(features, owner_order, [early[i % 2] for i in range(bands)]))
         packed = pack(features, owner_order, [late[i % 2] for i in range(bands)])
-        received, packed = lax.optimization_barrier((received, packed))
+        early_table, late_table = (
+            lax.dynamic_index_in_dim(tables, lax.rem(lax.axis_index("rows"), 2), 0, keepdims=False)
+            for tables in (
+                unpack_table((early, shared), (later, -HALO), wide, bands, frames, height),
+                unpack_table((late, middle), (-HALO, soon - HALO), rest, bands, frames, height),
+            )
+        )
+        received, packed, scalars, vectors, early_table, late_table = lax.optimization_barrier(
+            (received, packed, scalars, vectors, early_table, late_table)
+        )
         received_late = exchange(packed)
         halo = lax.ppermute(
             columns_of(received, soon, 0, HALO), "rows", [(i, i ^ 1) for i in range(bands)]
         )
         half, kept = stage(
-            owner_order,
-            frame_counts,
+            scalars,
             [slabbed(received), slabbed(halo)],
-            unpack_table((early, shared), (later, -HALO), wide, bands, frames, height),
+            early_table,
             None,
             None,
             kernels,
@@ -364,10 +410,9 @@
             **common,
         )
         (result,) = stage(
-            owner_order,
-            frame_counts,
+            scalars,
             [slabbed(received_late), slabbed(columns_of(received, soon, soon - HALO, soon))],
-            unpack_table((late, middle), (-HALO, soon - HALO), rest, bands, frames, height),
+            late_table,
             kept,
             half,
             kernels,
@@ -390,10 +435,9 @@
         right = lax.ppermute(columns_of(received, band, 0, HALO), "rows", [(j, i) for i, j in up])
         held = ([own], [list(range(-HALO, 0))], [list(range(band, band + HALO))])
         (result,) = stage(
-            owner_order,
-            frame_counts,
+            scalars,
             [slabbed(received), slabbed(left), slabbed(right)],
-            unpack_table(held, (-HALO,), band + 2 * HALO, bands, frames, height),
+            unpack_table(held, (-HALO,), band + 2 * HALO, bands, frames, height)[0],
             None,
             None,
             kernels,

time: 89.3 us -> 78.5 us (0.88)
  local copies, waits for them, and re-layouts: 13 us -> 4.67 us
  waiting for transfers between devices: 17.2 us -> 13 us
  Pallas kernels: 48.5 us -> 49.5 us
    unnamed x18 -> x0, local copies, waits for them, and re-layouts: 7.15 us -> none
    reshape x4 -> x0, local copies, waits for them, and re-layouts: 5.06 us -> none  [per_device(): v.reshape(1, channels)]
    all_to_all x2, waiting for transfers between devices: 17.2 us -> 13 us  [exchange(): lax.all_to_all(packed, ('tm', 'rows'), split_axis=0, concat_axis=0, tiled...]
    another operation x0 -> x4, local copies, waits for them, and re-layouts: none -> 2.73 us  [per_device(): vectors = jnp.stack([first_gain, first_bias, second_gain, second_bias])]
    squeeze x0 -> x2, local copies, waits for them, and re-layouts: none -> 1.9 us  [per_device(): lax.dynamic_index_in_dim(tables, lax.rem(lax.axis_index('rows'), 2), 0, k...]
    pallas_call x4, Pallas kernels: 48.5 us -> 49.5 us  [the longest x2 42.1 us: stage(): pl.pallas_call(kernel, grid_spec=pltpu.PrefetchScalarGridSpec(num_scalar_...]
  transfers between devices with their start and end apart: 3 -> 3, of which waited for: 1 -> 1; matrix products, arithmetic and copies ran while one was open for 6% -> 7% of each run, Pallas kernels for 29% -> 33%
where the time goes in v1:
time: 78.5 us; the launch traced here: 78 us
  Pallas kernels  49.5 us (63%)
  waiting for transfers between devices  13 us (17%)
  starting transfers between devices  10 us (13%)
  local copies, waits for them, and re-layouts  4.67 us (6%)
    pallas_call x2, Pallas kernels, stage(): pl.pallas_call(kernel, grid_spec=pltpu.PrefetchScalarGridSpec(num_scalar_...  42.1 us
    all_to_all x2, waiting for transfers between devices, exchange(): lax.all_to_all(packed, ('tm', 'rows'), split_axis=0, concat_axis=0, tiled...  13 us
    all_to_all x2, starting transfers between devices, exchange(): lax.all_to_all(packed, ('tm', 'rows'), split_axis=0, concat_axis=0, tiled...  9.93 us
    pallas_call x2, Pallas kernels, pack(): pl.pallas_call(kernel, grid_spec=pltpu.PrefetchScalarGridSpec(num_scalar_...  7.41 us
    another operation x4, local copies, waits for them, and re-layouts, per_device(): vectors = jnp.stack([first_gain, first_bias, second_gain, second_bias])  2.73 us
    squeeze x2, local copies, waits for them, and re-layouts, per_device(): lax.dynamic_index_in_dim(tables, lax.rem(lax.axis_index('rows'), 2), 0, k...  1.9 us
  transfers between devices with their start and end apart: 3, of which 1 were waited for; matrix products, arithmetic and copies ran while one was open for 7% of the time, Pallas kernels for 33%

profile of v1, /device:TPU:0, one launch (start us, length us, event | category | flops | bytes accessed | tf_op | source)
XLA Modules:
  0.0 78.0 jit_solution(6101908679041367975)
XLA Ops:
  0.0 3.8 %shard_map.127 = bf16[4,256,384]{2,1,0:T(8,128)(2,1)} custom-call(s32[4]{0:T(128)} %order_ref.3, bf16[256,384]{1,0:T(8,128)(2,1)} %constant.26.clone.table_ref, bf16[4,384,384]{2,1,0:T(8,128)(2,1)} %bitcast.25), custom_call_target="tpu_custom_call" | custom-call | tf_op jit(solution)/shard_map/pallas_call | solution.py:50
  3.8 7.3 %all-to-all-start = ((bf16[32,32,384]{2,1,0:T(8,128)(2,1)}), bf16[32,32,384]{2,1,0:T(8,128)(2,1)S(1)}, u32[]{:S(2)}, u32[]{:S(2)}) async-start(bf16[32,32,384]{2,1,0:T(8,128)(2,1)} %bitcast.27), calls=%async_computation | async-start | bytes 1572864 | tf_op jit(solution)/shard_map/all_to_all | solution.py:338
  11.1 0.7 stack.15
  11.8 0.7 stack.16
  12.5 0.7 stack.17
  13.2 0.7 stack.18
  13.9 3.6 %shard_map.128 = bf16[4,192,384]{2,1,0:T(8,128)(2,1)} custom-call(s32[4]{0:T(128)} %order_ref.3, bf16[192,384]{1,0:T(8,128)(2,1)} %constant.27.clone.table_ref, bf16[4,384,384]{2,1,0:T(8,128)(2,1)} %bitcast.26), custom_call_target="tpu_custom_call" | custom-call | tf_op jit(solution)/shard_map/pallas_call | solution.py:50
  17.5 0.7 pad_add_fusion.refs_0_
  18.3 0.9 %dynamic-slice_bitcast_fusion.1.refs_3_ = bf16[256,256]{1,0:T(8,128)(2,1)S(1)} fusion(bf16[2,256,256]{2,1,0:T(8,128)(2,1)} %constant.29.clone, s32[]{:T(128)S(6)} %select_n.6), kind=kLoop, calls=%fused_computation.2 | loop fusion | bytes 262148 | tf_op jit(solution)/shard_map/jit(dynamic_index_in_dim)/squeeze | solution.py:382
  19.2 1.0 %dynamic-slice_bitcast_fusion.refs_3_ = bf16[320,384]{1,0:T(8,128)(2,1)S(1)} fusion(bf16[2,320,384]{2,1,0:T(8,128)(2,1)} %constant.28.clone, s32[]{:T(128)S(6)} %select_n.6), kind=kLoop, calls=%fused_computation | loop fusion | bytes 491524 | tf_op jit(solution)/shard_map/jit(dynamic_index_in_dim)/squeeze | solution.py:382
  20.2 12.9 %all-to-all-done = bf16[32,32,384]{2,1,0:T(8,128)(2,1)S(1)} async-done(((bf16[32,32,384]{2,1,0:T(8,128)(2,1)}), bf16[32,32,384]{2,1,0:T(8,128)(2,1)S(1)}, u32[]{:S(2)}, u32[]{:S(2)}) %all-to-all-start) | async-done | bytes 786464 | tf_op jit(solution)/shard_map/all_to_all | solution.py:338
  33.1 0.1 collective-permute-start
  33.2 2.6 %all-to-all-start.1 = ((bf16[32,24,384]{2,1,0:T(8,128)(2,1)}), bf16[32,24,384]{2,1,0:T(8,128)(2,1)S(1)}, u32[]{:S(2)}, u32[]{:S(2)}) async-start(bf16[32,24,384]{2,1,0:T(8,128)(2,1)} %bitcast.28), calls=%async_computation.1 | async-start | bytes 1179648 | tf_op jit(solution)/shard_map/all_to_all | solution.py:338
  35.9 0.0 collective-permute-done
  35.9 21.9 %shard_map.129 = (bf16[8,6,16,384]{3,2,1,0:T(8,128)(2,1)S(1)}, bf16[8,2,16,384]{3,2,1,0:T(8,128)(2,1)S(1)}) custom-call(s32[8]{0:T(128)S(1)} %pad_add_fusion.refs_0_, bf16[4,256,384]{2,1,0:T(8,128)(2,1)S(1)} %bitcast.21, bf16[4,64,384]{2,1,0:T(8,128)(2,1)S(1)} %bitcast.24, bf16[320,384]{1,0:T(8,128)(2,1)S(1)} %dynamic-slice_bitcast_fusion.refs_3_, ...), custom_call_target="tpu_custom_call" | custom-call | flops 14269022208 | bytes 20971520 | tf_op jit(solution)/shard_map/pallas_call | solution.py:322
  57.8 0.0 all-to-all-done.1
  57.8 20.2 %shard_map.130 = bf16[8,12,16,384]{3,2,1,0:T(8,128)(2,1)} custom-call(s32[8]{0:T(128)S(1)} %pad_add_fusion.refs_0_, bf16[4,192,384]{2,1,0:T(8,128)(2,1)S(1)} %bitcast.22, bf16[4,64,384]{2,1,0:T(8,128)(2,1)S(1)} %bitcast.23, bf16[256,256]{1,0:T(8,128)(2,1)S(1)} %dynamic-slice_bitcast_fusion.1.refs_3_, bf16[8,2,16,384]{3,2,1,0:T(8,128)(2,1)S(1)} %get-tuple-element.19.refs_4_, ...), custom_call_target="tpu_custom_call" | custom-call | flops 12230590464 | bytes 20971520 | tf_op jit(solution)/shard_map/pallas_call | solution.py:322
  (2 shorter events, 0.1 us)
Async XLA Ops:
  3.8 29.3 %all-to-all-start = ((bf16[32,32,384]{2,1,0:T(8,128)(2,1)}), bf16[32,32,384]{2,1,0:T(8,128)(2,1)S(1)}, u32[]{:S(2)}, u32[]{:S(2)}) async-start(bf16[32,32,384]{2,1,0:T(8,128)(2,1)} %bitcast.27), calls=%async_computation | async-start | bytes 1572864 | tf_op jit(solution)/shard_map/all_to_all | solution.py:338
  33.1 2.7 %collective-permute-start = (bf16[256,384]{1,0:T(8,128)(2,1)S(1)}, bf16[256,384]{1,0:T(8,128)(2,1)S(1)}, u32[]{:S(2)}, u32[]{:S(2)}) collective-permute-start(bf16[256,384]{1,0:T(8,128)(2,1)S(1)} %get-tuple-element.21), channel_id=1, source_target_pairs={{0,1},{1,0},{2,3},{3,2},{4,5},{5,4},{6,7},{7,6},{8,9},{9,8},{10,11... | collective-permute-start | bytes 589832 | tf_op jit(solution)/shard_map/ppermute | solution.py:392
  33.2 24.6 %all-to-all-start.1 = ((bf16[32,24,384]{2,1,0:T(8,128)(2,1)}), bf16[32,24,384]{2,1,0:T(8,128)(2,1)S(1)}, u32[]{:S(2)}, u32[]{:S(2)}) async-start(bf16[32,24,384]{2,1,0:T(8,128)(2,1)} %bitcast.28), calls=%async_computation.1 | async-start | bytes 1179648 | tf_op jit(solution)/shard_map/all_to_all | solution.py:338

commit v2 on v1

--- a/solution.py
+++ b/solution.py
@@ -103,31 +103,31 @@
             ]
 
 
-def group(frames, rows):
-    return max(g for g in range(1, frames + 1) if frames % g == 0 and (g == 1 or g * rows <= 640))
-
-
-def multiply(taps_ref, weights_ref, copies, near_ref, far_ref, rows, channels):
+def group(frames, rows, most):
+    sizes = [g for g in range(1, most + 1) if frames % g == 0]
+    return max(g for g in sizes if g == 1 or g * rows <= 640)
+
+
+def multiply(taps_ref, weights_ref, copies, near_ref, far_ref, rows, channels, beside_near, beside_far):
     frames, _, taps = taps_ref.shape
     near_ref[0, :rows] = jnp.zeros((rows, 2 * channels), jnp.float32)
     far_ref[:2, :rows] = jnp.zeros((2, rows, channels), jnp.float32)
 
-    def dots(count, sums_ref, skip, start, width):
-        size = group(count, rows)
-
-        @pl.loop(0, count // size)
-        def _(step):
-            operand = taps_ref[pl.ds(step * size, size), :rows].reshape(size * rows, taps)
+    def dots(count, sums_ref, skip, start, width, beside):
+        size = group(count, rows, count // 2)
+        for first in range(0, count, size):
+            operand = taps_ref[first : first + size, :rows].reshape(size * rows, taps)
             sums = jnp.dot(
                 operand, weights_ref[:, start : start + width], preferred_element_type=jnp.float32
             )
-            sums_ref[pl.ds(step * size + skip, size), :rows] = sums.reshape(size, rows, width)
+            sums_ref[first + skip : first + skip + size, :rows] = sums.reshape(size, rows, width)
+            beside(first, size, first + size == count)
 
     copies[0].wait()
     copies[1].wait()
-    dots(frames, near_ref, 1, 0, 2 * channels)
+    dots(frames, near_ref, 1, 0, 2 * channels, beside_near)
     copies[2].wait()
-    dots(frames - 2, far_ref, 2, 2 * channels, channels)
+    dots(frames - 2, far_ref, 2, 2 * channels, channels, beside_far)
 
 
 def added(near_ref, far_ref, frame, rows, channels):
@@ -229,20 +229,19 @@
             placed = permuted(table_ref[...], rows).reshape(-1, columns, height, channels)
             raw_ref[pl.ds(slab * placed.shape[0], placed.shape[0])] = placed
 
-        @pl.loop(0, frames)
-        def _(frame):
+        def prepare(frame):
             values = raw_ref[frame].reshape(columns * height, channels).astype(jnp.float32)
             spread(normalize(values, first_gain), taps_ref, frame, height)
 
-        multiply(taps_ref, weights_refs[0], copies[0], near_ref, far_ref, inner, channels)
-        place = lax.broadcasted_iota(jnp.int32, (inner, 1), 0)
-        outside = ((place < height) & first_edge) | ((place >= inner - height) & last_edge)
-
-        @pl.loop(0, frames)
-        def _(frame):
+        def hide(frame):
             hidden = added(near_ref, far_ref, frame, inner, channels) + first_bias
             hidden = hidden.astype(jnp.bfloat16).astype(jnp.float32)
-            active = jnp.where(outside, 0.0, normalize(hidden, second_gain))
+            active = normalize(hidden, second_gain)
+            if edges:
+                place = lax.broadcasted_iota(jnp.int32, (inner, 1), 0)
+                outside = (place < height) & first_edge
+                outside |= (place >= inner - height) & last_edge
+                active = jnp.where(outside, 0.0, active)
             if saved is not None or keeps:
                 active = active.reshape(fresh, height, channels)
                 active_ref[pl.ds(pick(new_at), fresh)] = active
@@ -254,11 +253,6 @@
                 active = active_ref[...].reshape(window * height, channels)
             spread(active, taps_ref, frame, height)
 
-        if joins:
-            held.wait()
-            moved.start()
-        multiply(taps_ref, weights_refs[1], copies[1], near_ref, far_ref, outer, channels)
-
         def write(frame):
             return pltpu.make_async_copy(
                 result_ref.at[frame],
@@ -266,8 +260,7 @@
                 written.at[frame],
             )
 
-        @pl.loop(0, frames)
-        def _(frame):
+        def finish(frame):
             center = raw_ref[frame, pl.ds(pick(center_at), made)].reshape(outer, channels)
             result = added(near_ref, far_ref, frame, outer, channels) + second_bias
             result = result + center.astype(jnp.float32)
@@ -276,6 +269,46 @@
             if joins:
                 write(frame).start()
 
+        done = {prepare: 0, hide: 0, finish: 0}
+
+        def through(work, stop, unrolled=True):
+            start, done[work] = done[work], max(done[work], min(stop, frames))
+            if unrolled:
+                for frame in range(start, done[work]):
+                    work(frame)
+            elif start < done[work]:
+                pl.loop(start, done[work])(work)
+
+        first_size = group(frames, inner, frames // 2)
+        second_size = group(frames, outer, frames // 2)
+        through(prepare, first_size, False)
+        multiply(
+            taps_ref,
+            weights_refs[0],
+            copies[0],
+            near_ref,
+            far_ref,
+            inner,
+            channels,
+            lambda first, size, last: through(prepare, first + 2 * size),
+            lambda first, size, last: through(hide, first if last else 0),
+        )
+        through(hide, second_size + 1, False)
+        if joins:
+            held.wait()
+            moved.start()
+        multiply(
+            taps_ref,
+            weights_refs[1],
+            copies[1],
+            near_ref,
+            far_ref,
+            outer,
+            channels,
+            lambda first, size, last: through(hide, frames),
+            lambda first, size, last: through(finish, first + 2 if last else 0),
+        )
+        through(finish, frames, False)
         if joins:
             moved.wait()
 

time: 78.5 us -> 75.5 us (0.962)
  Pallas kernels: 49.5 us -> 46.4 us
    pallas_call x2, Pallas kernels: 42.1 us -> 39 us  [stage(): pl.pallas_call(kernel, grid_spec=pltpu.PrefetchScalarGridSpec(num_scalar_...]
  transfers between devices with their start and end apart: 3 -> 3, of which waited for: 1 -> 1; matrix products, arithmetic and copies ran while one was open for 7% -> 7% of each run, Pallas kernels for 33% -> 32%
where the time goes in v2:
time: 75.5 us; the launch traced here: 75.1 us
  Pallas kernels  46.4 us (61%)
  waiting for transfers between devices  13 us (17%)
  starting transfers between devices  10 us (13%)
  local copies, waits for them, and re-layouts  4.67 us (6%)
  other arithmetic  0.76 us (1%)
    pallas_call x2, Pallas kernels, stage(): pl.pallas_call(kernel, grid_spec=pltpu.PrefetchScalarGridSpec(num_scalar_...  39 us
    all_to_all x2, waiting for transfers between devices, exchange(): lax.all_to_all(packed, ('tm', 'rows'), split_axis=0, concat_axis=0, tiled...  13 us
    all_to_all x2, starting transfers between devices, exchange(): lax.all_to_all(packed, ('tm', 'rows'), split_axis=0, concat_axis=0, tiled...  9.93 us
    pallas_call x2, Pallas kernels, pack(): pl.pallas_call(kernel, grid_spec=pltpu.PrefetchScalarGridSpec(num_scalar_...  7.41 us
    another operation x4, local copies, waits for them, and re-layouts, per_device(): vectors = jnp.stack([first_gain, first_bias, second_gain, second_bias])  2.73 us
    squeeze x2, local copies, waits for them, and re-layouts, per_device(): lax.dynamic_index_in_dim(tables, lax.rem(lax.axis_index('rows'), 2), 0, k...  1.9 us
  transfers between devices with their start and end apart: 3, of which 1 were waited for; matrix products, arithmetic and copies ran while one was open for 7% of the time, Pallas kernels for 32%

profile of v2, /device:TPU:0, one launch (start us, length us, event | category | flops | bytes accessed | tf_op | source)
XLA Modules:
  0.0 75.1 jit_solution(8901420726835247172)
XLA Ops:
  0.0 3.8 %shard_map.127 = bf16[4,256,384]{2,1,0:T(8,128)(2,1)} custom-call(s32[4]{0:T(128)} %order_ref.3, bf16[256,384]{1,0:T(8,128)(2,1)} %constant.26.clone.table_ref, bf16[4,384,384]{2,1,0:T(8,128)(2,1)} %bitcast.25), custom_call_target="tpu_custom_call" | custom-call | tf_op jit(solution)/shard_map/pallas_call | solution.py:50
  3.8 7.3 %all-to-all-start = ((bf16[32,32,384]{2,1,0:T(8,128)(2,1)}), bf16[32,32,384]{2,1,0:T(8,128)(2,1)S(1)}, u32[]{:S(2)}, u32[]{:S(2)}) async-start(bf16[32,32,384]{2,1,0:T(8,128)(2,1)} %bitcast.27), calls=%async_computation | async-start | bytes 1572864 | tf_op jit(solution)/shard_map/all_to_all | solution.py:371
  11.1 0.7 stack.15
  11.8 0.7 stack.16
  12.5 0.7 stack.17
  13.2 0.7 stack.18
  13.9 3.6 %shard_map.128 = bf16[4,192,384]{2,1,0:T(8,128)(2,1)} custom-call(s32[4]{0:T(128)} %order_ref.3, bf16[192,384]{1,0:T(8,128)(2,1)} %constant.27.clone.table_ref, bf16[4,384,384]{2,1,0:T(8,128)(2,1)} %bitcast.26), custom_call_target="tpu_custom_call" | custom-call | tf_op jit(solution)/shard_map/pallas_call | solution.py:50
  17.5 0.7 pad_add_fusion.refs_0_
  18.3 0.9 %dynamic-slice_bitcast_fusion.1.refs_3_ = bf16[256,256]{1,0:T(8,128)(2,1)S(1)} fusion(bf16[2,256,256]{2,1,0:T(8,128)(2,1)} %constant.29.clone, s32[]{:T(128)S(6)} %select_n.6), kind=kLoop, calls=%fused_computation.2 | loop fusion | bytes 262148 | tf_op jit(solution)/shard_map/jit(dynamic_index_in_dim)/squeeze | solution.py:415
  19.2 1.0 %dynamic-slice_bitcast_fusion.refs_3_ = bf16[320,384]{1,0:T(8,128)(2,1)S(1)} fusion(bf16[2,320,384]{2,1,0:T(8,128)(2,1)} %constant.28.clone, s32[]{:T(128)S(6)} %select_n.6), kind=kLoop, calls=%fused_computation | loop fusion | bytes 491524 | tf_op jit(solution)/shard_map/jit(dynamic_index_in_dim)/squeeze | solution.py:415
  20.2 12.9 %all-to-all-done = bf16[32,32,384]{2,1,0:T(8,128)(2,1)S(1)} async-done(((bf16[32,32,384]{2,1,0:T(8,128)(2,1)}), bf16[32,32,384]{2,1,0:T(8,128)(2,1)S(1)}, u32[]{:S(2)}, u32[]{:S(2)}) %all-to-all-start) | async-done | bytes 786464 | tf_op jit(solution)/shard_map/all_to_all | solution.py:371
  33.1 0.1 collective-permute-start
  33.2 2.6 %all-to-all-start.1 = ((bf16[32,24,384]{2,1,0:T(8,128)(2,1)}), bf16[32,24,384]{2,1,0:T(8,128)(2,1)S(1)}, u32[]{:S(2)}, u32[]{:S(2)}) async-start(bf16[32,24,384]{2,1,0:T(8,128)(2,1)} %bitcast.28), calls=%async_computation.1 | async-start | bytes 1179648 | tf_op jit(solution)/shard_map/all_to_all | solution.py:371
  35.9 0.0 collective-permute-done
  35.9 20.2 %shard_map.129 = (bf16[8,6,16,384]{3,2,1,0:T(8,128)(2,1)S(1)}, bf16[8,2,16,384]{3,2,1,0:T(8,128)(2,1)S(1)}) custom-call(s32[8]{0:T(128)S(1)} %pad_add_fusion.refs_0_, bf16[4,256,384]{2,1,0:T(8,128)(2,1)S(1)} %bitcast.21, bf16[4,64,384]{2,1,0:T(8,128)(2,1)S(1)} %bitcast.24, bf16[320,384]{1,0:T(8,128)(2,1)S(1)} %dynamic-slice_bitcast_fusion.refs_3_, ...), custom_call_target="tpu_custom_call" | custom-call | flops 14269022208 | bytes 20971520 | tf_op jit(solution)/shard_map/pallas_call | solution.py:355
  56.1 0.0 all-to-all-done.1
  56.1 18.8 %shard_map.130 = bf16[8,12,16,384]{3,2,1,0:T(8,128)(2,1)} custom-call(s32[8]{0:T(128)S(1)} %pad_add_fusion.refs_0_, bf16[4,192,384]{2,1,0:T(8,128)(2,1)S(1)} %bitcast.22, bf16[4,64,384]{2,1,0:T(8,128)(2,1)S(1)} %bitcast.23, bf16[256,256]{1,0:T(8,128)(2,1)S(1)} %dynamic-slice_bitcast_fusion.1.refs_3_, bf16[8,2,16,384]{3,2,1,0:T(8,128)(2,1)S(1)} %get-tuple-element.19.refs_4_, ...), custom_call_target="tpu_custom_call" | custom-call | flops 12230590464 | bytes 20971520 | tf_op jit(solution)/shard_map/pallas_call | solution.py:355
  (2 shorter events, 0.1 us)
Async XLA Ops:
  3.8 29.3 %all-to-all-start = ((bf16[32,32,384]{2,1,0:T(8,128)(2,1)}), bf16[32,32,384]{2,1,0:T(8,128)(2,1)S(1)}, u32[]{:S(2)}, u32[]{:S(2)}) async-start(bf16[32,32,384]{2,1,0:T(8,128)(2,1)} %bitcast.27), calls=%async_computation | async-start | bytes 1572864 | tf_op jit(solution)/shard_map/all_to_all | solution.py:371
  33.1 2.7 %collective-permute-start = (bf16[256,384]{1,0:T(8,128)(2,1)S(1)}, bf16[256,384]{1,0:T(8,128)(2,1)S(1)}, u32[]{:S(2)}, u32[]{:S(2)}) collective-permute-start(bf16[256,384]{1,0:T(8,128)(2,1)S(1)} %get-tuple-element.21), channel_id=1, source_target_pairs={{0,1},{1,0},{2,3},{3,2},{4,5},{5,4},{6,7},{7,6},{8,9},{9,8},{10,11... | collective-permute-start | bytes 589832 | tf_op jit(solution)/shard_map/ppermute | solution.py:425
  33.2 22.9 %all-to-all-start.1 = ((bf16[32,24,384]{2,1,0:T(8,128)(2,1)}), bf16[32,24,384]{2,1,0:T(8,128)(2,1)S(1)}, u32[]{:S(2)}, u32[]{:S(2)}) async-start(bf16[32,24,384]{2,1,0:T(8,128)(2,1)} %bitcast.28), calls=%async_computation.1 | async-start | bytes 1179648 | tf_op jit(solution)/shard_map/all_to_all | solution.py:371

commit v3 on v2

--- a/solution.py
+++ b/solution.py
@@ -32,7 +32,7 @@
     places = np.arange(frames * height) * width + columns[:, :, None]
     places = np.where(((columns >= 0) & (columns < width))[:, :, None], places, -1).reshape(-1)
 
-    def kernel(order_ref, table_ref, features_ref, out_ref, table, sources, arrived):
+    def kernel(order_ref, table_ref, features_ref, out_ref, table, sources, packed, arrived, left):
         fetched = pltpu.make_async_copy(table_ref, table, arrived.at[clips])
         copies = [
             pltpu.make_async_copy(
@@ -45,7 +45,10 @@
         fetched.wait()
         for slot, copy in enumerate(copies):
             copy.wait()
-            out_ref[slot] = permuted(table[...], sources[slot])
+            packed[slot] = permuted(table[...], sources[slot])
+            pltpu.make_async_copy(packed.at[slot], out_ref.at[slot], left.at[slot]).start()
+        for slot in range(clips):
+            pltpu.make_async_copy(packed.at[slot], out_ref.at[slot], left.at[slot]).wait()
 
     packed = pl.pallas_call(
         kernel,
@@ -53,11 +56,13 @@
             num_scalar_prefetch=1,
             grid=(1,),
             in_specs=[ANYWHERE] * 2,
-            out_specs=WHOLE,
+            out_specs=ANYWHERE,
             scratch_shapes=[
                 pltpu.VMEM((len(places), rows), jnp.bfloat16),
                 pltpu.VMEM((clips, rows, channels), jnp.bfloat16),
+                pltpu.VMEM((clips, len(places), channels), jnp.bfloat16),
                 pltpu.SemaphoreType.DMA((clips + 1,)),
+                pltpu.SemaphoreType.DMA((clips,)),
             ],
         ),
         out_shape=jax.ShapeDtypeStruct((clips, len(places), channels), features.dtype),
@@ -94,11 +99,12 @@
     above = jnp.where(place == 0, 0.0, pltpu.roll(active, 1, 0))
     below = jnp.where(place == height - 1, 0.0, pltpu.roll(active, rows - 1, 0))
     kept = rows - 2 * height
+    first = frame * kept if isinstance(frame, int) else pl.multiple_of(frame * kept, kept)
     for row_tap, shifted in enumerate((above, active, below)):
         narrow = shifted.astype(jnp.bfloat16)
         for column_tap in range(3):
             at = (row_tap * 3 + column_tap) * channels
-            taps_ref[frame, :kept, at : at + channels] = narrow[
+            taps_ref[pl.ds(first, kept), at : at + channels] = narrow[
                 column_tap * height : column_tap * height + kept
             ]
 
@@ -109,14 +115,14 @@
 
 
 def multiply(taps_ref, weights_ref, copies, near_ref, far_ref, rows, channels, beside_near, beside_far):
-    frames, _, taps = taps_ref.shape
+    frames = far_ref.shape[0]
     near_ref[0, :rows] = jnp.zeros((rows, 2 * channels), jnp.float32)
     far_ref[:2, :rows] = jnp.zeros((2, rows, channels), jnp.float32)
 
     def dots(count, sums_ref, skip, start, width, beside):
         size = group(count, rows, count // 2)
         for first in range(0, count, size):
-            operand = taps_ref[first : first + size, :rows].reshape(size * rows, taps)
+            operand = taps_ref[first * rows : (first + size) * rows]
             sums = jnp.dot(
                 operand, weights_ref[:, start : start + width], preferred_element_type=jnp.float32
             )
@@ -334,7 +340,7 @@
         pltpu.VMEM((taps, 3 * channels), jnp.bfloat16),
         pltpu.VMEM((taps, 3 * channels), jnp.bfloat16),
         pltpu.VMEM((frames, columns, height, channels), jnp.bfloat16),
-        pltpu.VMEM((frames, most, taps), jnp.bfloat16),
+        pltpu.VMEM((frames * most, taps), jnp.bfloat16),
         pltpu.VMEM((frames + 1, most, 2 * channels), jnp.float32),
         pltpu.VMEM((frames, most, channels), jnp.float32),
         pltpu.VMEM((window, height, channels), jnp.float32),
@@ -349,7 +355,7 @@
     held = sum(
         int(np.prod(ref.shape)) * jnp.dtype(ref.dtype).itemsize
         for ref in scratch
-        if len(ref.shape) > 2 or ref.shape[0] == taps
+        if len(ref.shape) > 1 and ref.shape != (2, 3)
     )
     flops = 2 * 3 * taps * channels * frames * (inner + outer)
     return pl.pallas_call(

time: 75.5 us -> 75.4 us (level)
  no operation moved by 1% of the time
where the time goes in v3:
time: 75.4 us; the launch traced here: 74.9 us
  Pallas kernels  46.1 us (61%)
  waiting for transfers between devices  13.1 us (17%)
  starting transfers between devices  10 us (13%)
  local copies, waits for them, and re-layouts  4.67 us (6%)
  other arithmetic  0.76 us (1%)
    pallas_call x2, Pallas kernels, stage(): pl.pallas_call(kernel, grid_spec=pltpu.PrefetchScalarGridSpec(num_scalar_...  39 us
    all_to_all x2, waiting for transfers between devices, exchange(): lax.all_to_all(packed, ('tm', 'rows'), split_axis=0, concat_axis=0, tiled...  13.1 us
    all_to_all x2, starting transfers between devices, exchange(): lax.all_to_all(packed, ('tm', 'rows'), split_axis=0, concat_axis=0, tiled...  9.93 us
    pallas_call x2, Pallas kernels, pack(): pl.pallas_call(kernel, grid_spec=pltpu.PrefetchScalarGridSpec(num_scalar_...  7.12 us
    another operation x4, local copies, waits for them, and re-layouts, per_device(): vectors = jnp.stack([first_gain, first_bias, second_gain, second_bias])  2.73 us
    squeeze x2, local copies, waits for them, and re-layouts, per_device(): lax.dynamic_index_in_dim(tables, lax.rem(lax.axis_index('rows'), 2), 0, k...  1.9 us
  transfers between devices with their start and end apart: 3, of which 1 were waited for; matrix products, arithmetic and copies ran while one was open for 7% of the time, Pallas kernels for 32%

profile of v3, /device:TPU:0, one launch (start us, length us, event | category | flops | bytes accessed | tf_op | source)
XLA Modules:
  0.0 74.9 jit_solution(13836795687031327144)
XLA Ops:
  0.0 3.6 %shard_map.127 = bf16[4,256,384]{2,1,0:T(8,128)(2,1)} custom-call(s32[4]{0:T(128)} %order_ref.3, bf16[256,384]{1,0:T(8,128)(2,1)} %constant.26.clone.table_ref, bf16[4,384,384]{2,1,0:T(8,128)(2,1)} %bitcast.25), custom_call_target="tpu_custom_call" | custom-call | tf_op jit(solution)/shard_map/pallas_call | solution.py:53
  3.7 7.3 %all-to-all-start = ((bf16[32,32,384]{2,1,0:T(8,128)(2,1)}), bf16[32,32,384]{2,1,0:T(8,128)(2,1)S(1)}, u32[]{:S(2)}, u32[]{:S(2)}) async-start(bf16[32,32,384]{2,1,0:T(8,128)(2,1)} %bitcast.27), calls=%async_computation | async-start | bytes 1572864 | tf_op jit(solution)/shard_map/all_to_all | solution.py:377
  11.0 0.7 stack.15
  11.7 0.7 stack.16
  12.3 0.7 stack.17
  13.0 0.7 stack.18
  13.7 3.5 %shard_map.128 = bf16[4,192,384]{2,1,0:T(8,128)(2,1)} custom-call(s32[4]{0:T(128)} %order_ref.3, bf16[192,384]{1,0:T(8,128)(2,1)} %constant.27.clone.table_ref, bf16[4,384,384]{2,1,0:T(8,128)(2,1)} %bitcast.26), custom_call_target="tpu_custom_call" | custom-call | tf_op jit(solution)/shard_map/pallas_call | solution.py:53
  17.2 0.7 pad_add_fusion.refs_0_
  18.0 0.9 %dynamic-slice_bitcast_fusion.1.refs_3_ = bf16[256,256]{1,0:T(8,128)(2,1)S(1)} fusion(bf16[2,256,256]{2,1,0:T(8,128)(2,1)} %constant.29.clone, s32[]{:T(128)S(6)} %select_n.6), kind=kLoop, calls=%fused_computation.2 | loop fusion | bytes 262148 | tf_op jit(solution)/shard_map/jit(dynamic_index_in_dim)/squeeze | solution.py:421
  18.9 1.0 %dynamic-slice_bitcast_fusion.refs_3_ = bf16[320,384]{1,0:T(8,128)(2,1)S(1)} fusion(bf16[2,320,384]{2,1,0:T(8,128)(2,1)} %constant.28.clone, s32[]{:T(128)S(6)} %select_n.6), kind=kLoop, calls=%fused_computation | loop fusion | bytes 491524 | tf_op jit(solution)/shard_map/jit(dynamic_index_in_dim)/squeeze | solution.py:421
  19.9 13.1 %all-to-all-done = bf16[32,32,384]{2,1,0:T(8,128)(2,1)S(1)} async-done(((bf16[32,32,384]{2,1,0:T(8,128)(2,1)}), bf16[32,32,384]{2,1,0:T(8,128)(2,1)S(1)}, u32[]{:S(2)}, u32[]{:S(2)}) %all-to-all-start) | async-done | bytes 786464 | tf_op jit(solution)/shard_map/all_to_all | solution.py:377
  33.0 0.1 collective-permute-start
  33.1 2.6 %all-to-all-start.1 = ((bf16[32,24,384]{2,1,0:T(8,128)(2,1)}), bf16[32,24,384]{2,1,0:T(8,128)(2,1)S(1)}, u32[]{:S(2)}, u32[]{:S(2)}) async-start(bf16[32,24,384]{2,1,0:T(8,128)(2,1)} %bitcast.28), calls=%async_computation.1 | async-start | bytes 1179648 | tf_op jit(solution)/shard_map/all_to_all | solution.py:377
  35.7 0.0 collective-permute-done
  35.7 20.2 %shard_map.129 = (bf16[8,6,16,384]{3,2,1,0:T(8,128)(2,1)S(1)}, bf16[8,2,16,384]{3,2,1,0:T(8,128)(2,1)S(1)}) custom-call(s32[8]{0:T(128)S(1)} %pad_add_fusion.refs_0_, bf16[4,256,384]{2,1,0:T(8,128)(2,1)S(1)} %bitcast.21, bf16[4,64,384]{2,1,0:T(8,128)(2,1)S(1)} %bitcast.24, bf16[320,384]{1,0:T(8,128)(2,1)S(1)} %dynamic-slice_bitcast_fusion.refs_3_, ...), custom_call_target="tpu_custom_call" | custom-call | flops 14269022208 | bytes 20971520 | tf_op jit(solution)/shard_map/pallas_call | solution.py:361
  55.9 0.0 all-to-all-done.1
  55.9 18.8 %shard_map.130 = bf16[8,12,16,384]{3,2,1,0:T(8,128)(2,1)} custom-call(s32[8]{0:T(128)S(1)} %pad_add_fusion.refs_0_, bf16[4,192,384]{2,1,0:T(8,128)(2,1)S(1)} %bitcast.22, bf16[4,64,384]{2,1,0:T(8,128)(2,1)S(1)} %bitcast.23, bf16[256,256]{1,0:T(8,128)(2,1)S(1)} %dynamic-slice_bitcast_fusion.1.refs_3_, bf16[8,2,16,384]{3,2,1,0:T(8,128)(2,1)S(1)} %get-tuple-element.19.refs_4_, ...), custom_call_target="tpu_custom_call" | custom-call | flops 12230590464 | bytes 20971520 | tf_op jit(solution)/shard_map/pallas_call | solution.py:361
  (2 shorter events, 0.1 us)
Async XLA Ops:
  3.7 29.3 %all-to-all-start = ((bf16[32,32,384]{2,1,0:T(8,128)(2,1)}), bf16[32,32,384]{2,1,0:T(8,128)(2,1)S(1)}, u32[]{:S(2)}, u32[]{:S(2)}) async-start(bf16[32,32,384]{2,1,0:T(8,128)(2,1)} %bitcast.27), calls=%async_computation | async-start | bytes 1572864 | tf_op jit(solution)/shard_map/all_to_all | solution.py:377
  33.0 2.7 %collective-permute-start = (bf16[256,384]{1,0:T(8,128)(2,1)S(1)}, bf16[256,384]{1,0:T(8,128)(2,1)S(1)}, u32[]{:S(2)}, u32[]{:S(2)}) collective-permute-start(bf16[256,384]{1,0:T(8,128)(2,1)S(1)} %get-tuple-element.21), channel_id=1, source_target_pairs={{0,1},{1,0},{2,3},{3,2},{4,5},{5,4},{6,7},{7,6},{8,9},{9,8},{10,11... | collective-permute-start | bytes 589832 | tf_op jit(solution)/shard_map/ppermute | solution.py:431
  33.1 22.9 %all-to-all-start.1 = ((bf16[32,24,384]{2,1,0:T(8,128)(2,1)}), bf16[32,24,384]{2,1,0:T(8,128)(2,1)S(1)}, u32[]{:S(2)}, u32[]{:S(2)}) async-start(bf16[32,24,384]{2,1,0:T(8,128)(2,1)} %bitcast.28), calls=%async_computation.1 | async-start | bytes 1179648 | tf_op jit(solution)/shard_map/all_to_all | solution.py:377
